TPU v7x, 256 devices: a whole 4x4x8 slice. The times are simulated.
256 devices in a mesh: dp: 4 (over z_lo), ep: 64 (over x, y, z_hi, core).
Axes of the slice: x: 4, y: 4, z: 8 (z_hi: 2, z_lo: 4; z = z_hi * 4 + z_lo), core: 2. Of those that a mesh axis runs over, the one named last changes fastest.
Arguments:
- lengths: int32 [1536], P(('dp', 'ep')), may hold values from 0 to 62, as said below
- send_slots: int32 [256, 4, 1], P(('dp', 'ep')), may hold values from 0 to 6, as said below
- recv_slots: int32 [256, 4, 1], P(('dp', 'ep')), may hold values from 0 to 6, as said below
- latent_cache: bfloat16 [1536, 64, 576], P(('dp', 'ep')), may hold values from -5 to 5
- queries: bfloat16 [2, 1536, 64, 576], P(None, ('dp', 'ep')), may hold values from -24 to 24
- newest_kv: bfloat16 [2, 1536, 576], P(None, ('dp', 'ep')), may hold values from -5 to 5
- hidden_rows: bfloat16 [1536, 7168], P(('dp', 'ep')), may hold values from -6 to 6
- route_ids: int32 [2, 64, 24, 8], P(None, 'ep'), may hold values from 0 to 63, all different within a row; in each aligned block of 6 rows (0 to 5, 6 to 11, ..., all dimensions but the last counted through in order) at most 2 rows name the same one
- route_gates: int32 [2, 64, 24, 8], P(None, 'ep'), may hold values from 1 to 15
- w_gate: bfloat16 [64, 7168, 1024], P('ep', None, 'dp'), may hold values from -0.0625 to 0.0625
- w_up: bfloat16 [64, 7168, 1024], P('ep', None, 'dp'), may hold values from -0.0625 to 0.0625
- w_down: bfloat16 [64, 1024, 7168], P('ep', 'dp'), may hold values from -0.1875 to 0.1875
Outputs:
- attention: bfloat16 [2, 1536, 64, 512], P(None, ('dp', 'ep'))
- final_rows: bfloat16 [1536, 7168], P(('dp', 'ep'))
Inputs may be any that keep to these rules, and one draw needn't show every extreme that they name: `lengths`: each index of ep has two ranks of dp with every slot live and two with one empty slot; live slots hold 1 to 62 positions, and 62 is reached in every index of ep. `send_slots`: in each index of ep the two full ranks each send one live request to one of the two other ranks, a different one each; at most 1 moves between two devices. `recv_slots`: entries describe the same moves as send_slots, entry m for entry m; a request lands in a slot empty before the move. `route_ids`: the 6 rows of one device name one expert at most 2 times.
All inputs are finite; a program needn't handle non-finite values.
Results may differ from a plain program's by a relative error of at most 0.018.
Values may be sent and summed in bfloat16 or wider, within the bound.
No kernel may reach another device: no remote copies, remote signals or barrier semaphores. Data moves between devices by JAX's collectives and lax.ppermute only.
A program may use at most 128 MiB of HBM per device.

v0:
```python
import jax
import jax.numpy as jnp
from jax import lax
from jax.sharding import PartitionSpec as P

LAT = 512


softmax_scale = 192.0 ** (-0.5)
route_scale = 2.5
norm_eps = 1e-06


def normed_rows(hidden):
    values = hidden.astype(jnp.float32)
    inverse = lax.rsqrt(jnp.mean(values * values, axis=1, keepdims=True) + norm_eps)
    return (values * inverse).astype(jnp.bfloat16)


def decode_pass(cache_rows, queries_now, newest, counts):
    positions = lax.broadcasted_iota(jnp.int32, cache_rows.shape[:2], 1)
    is_live = counts > 0
    placed = (positions == counts[:, None]) & is_live[:, None]
    cache_rows = jnp.where(placed[:, :, None], newest[:, None, :], cache_rows)
    scores = (
        jnp.einsum("nhk,ntk->nht", queries_now, cache_rows, preferred_element_type=jnp.float32)
        * softmax_scale
    )
    usable = positions <= counts[:, None]
    scores = jnp.where(usable[:, None, :], scores, -1e30)
    peak_score = jnp.max(scores, axis=2, keepdims=True)
    raised = jnp.exp(scores - peak_score)
    chances = (raised / jnp.sum(raised, axis=2, keepdims=True)).astype(jnp.bfloat16)
    output = jnp.einsum(
        "nht,ntl->nhl", chances, cache_rows[:, :, :LAT], preferred_element_type=jnp.float32
    )
    output = jnp.where(is_live[:, None, None], output, 0.0).astype(jnp.bfloat16)
    return (output, cache_rows)


def expert_rows(gathered_rows, gate_local, up_local, down_local):
    gate_val = jnp.dot(gathered_rows, gate_local, preferred_element_type=jnp.float32)
    up_val = jnp.dot(gathered_rows, up_local, preferred_element_type=jnp.float32)
    inner_rows = (jax.nn.silu(gate_val) * up_val).astype(jnp.bfloat16)
    return jnp.dot(inner_rows, down_local, preferred_element_type=jnp.float32).astype(jnp.bfloat16)


def route_tables(expert_ids, gate_values, devices, per_device, experts):
    rows_total, fanout = expert_ids.shape
    per_rows = rows_total // devices
    gate_float = gate_values.astype(jnp.float32)
    weights = route_scale * gate_float / jnp.sum(gate_float, axis=1, keepdims=True)
    grouped = expert_ids.reshape(devices, per_rows * fanout)
    expert_hits = (
        grouped[:, :, None] == lax.broadcasted_iota(jnp.int32, (1, 1, experts), 2)
    ).astype(jnp.int32)
    ranking = jnp.sum(jnp.cumsum(expert_hits, axis=1) * expert_hits, axis=2) - 1
    anchor = lax.broadcasted_iota(jnp.int32, grouped.shape, 0)
    target = (grouped * (devices * per_device) + anchor * per_device + ranking).reshape(-1)
    slot_width = experts * devices * per_device
    slot_hits = (target[:, None] == lax.broadcasted_iota(jnp.int32, (1, slot_width), 1)).astype(
        jnp.float32
    )
    token_of = lax.broadcasted_iota(jnp.int32, (rows_total * fanout, 1), 0) // fanout
    token_hits = (token_of == lax.broadcasted_iota(jnp.int32, (1, rows_total), 1)).astype(
        jnp.float32
    )
    packing = jnp.dot(slot_hits.T, token_hits).astype(jnp.bfloat16)
    combine = jnp.dot(
        (token_hits * weights.reshape(-1, 1)).T, slot_hits, precision=lax.Precision.HIGHEST
    )
    return (packing, combine)


def routed_layer(hidden, column_ids, column_gates, gate_local, up_local, down_local):
    slot_count, model_width = hidden.shape
    fanout = column_ids.shape[1]
    devices = lax.axis_size("dp")
    experts = lax.axis_size("ep")
    per_device = max(2, slot_count * fanout // experts)
    normed = normed_rows(hidden)
    column = lax.all_gather(normed, "dp", axis=0, tiled=True)
    packing, combine = route_tables(column_ids, column_gates, devices, per_device, experts)
    outgoing = jnp.dot(packing, column, preferred_element_type=jnp.float32).astype(jnp.bfloat16)
    outgoing = outgoing.reshape(experts, devices * per_device, model_width)
    received = lax.all_to_all(outgoing, "ep", split_axis=0, concat_axis=0, tiled=True)
    partial_value = expert_rows(received.reshape(-1, model_width), gate_local, up_local, down_local)
    returned = lax.all_to_all(
        partial_value.reshape(received.shape), "ep", split_axis=0, concat_axis=0, tiled=True
    )
    blended = jnp.dot(
        combine,
        returned.reshape(-1, model_width).astype(jnp.float32),
        precision=lax.Precision.HIGHEST,
    )
    addition = lax.psum_scatter(
        blended.astype(jnp.bfloat16), "dp", scatter_dimension=0, tiled=True
    ).astype(jnp.float32)
    return (hidden.astype(jnp.float32) + addition).astype(jnp.bfloat16)


def body(
    lengths,
    send_slots,
    recv_slots,
    latent_cache,
    queries,
    newest_kv,
    hidden_rows,
    route_ids,
    route_gates,
    w_gate,
    w_up,
    w_down,
):
    slot_count = lengths.shape[0]
    model_width = hidden_rows.shape[1]
    gate_local = w_gate[0]
    up_local = w_up[0]
    down_local = w_down[0]
    first_att, cache_now = decode_pass(latent_cache, queries[0], newest_kv[0], lengths)
    rows_one = routed_layer(
        hidden_rows, route_ids[0, 0], route_gates[0, 0], gate_local, up_local, down_local
    )
    counts_one = jnp.where(lengths > 0, lengths + 1, 0)
    send_row = send_slots[0]
    recv_row = recv_slots[0]
    leaving = send_row < slot_count
    chosen = jnp.minimum(send_row, slot_count - 1)
    local_slots = lax.broadcasted_iota(jnp.int32, (slot_count, 1), 0)
    vacated = jnp.any(send_row.reshape(1, -1) == local_slots, axis=1)
    landing = recv_row.reshape(1, -1) == local_slots
    incoming = jnp.any(landing, axis=1)
    source_item = jnp.argmax(landing.astype(jnp.int32), axis=1)
    kept_rows = jnp.where(vacated[:, None], jnp.zeros_like(rows_one), rows_one)
    rows_out = jnp.where(leaving[:, :, None], rows_one[chosen], jnp.zeros_like(rows_one[chosen]))
    stale_cache = cache_now[chosen]
    cache_out = jnp.where(leaving[:, :, None, None], stale_cache, jnp.zeros_like(stale_cache))
    count_out = jnp.where(leaving, counts_one[chosen], 0).astype(jnp.bfloat16)
    cache_in, rows_in, count_in = (
        lax.all_to_all(cache_out, "dp", split_axis=0, concat_axis=0, tiled=True),
        lax.all_to_all(rows_out, "dp", split_axis=0, concat_axis=0, tiled=True),
        lax.all_to_all(count_out, "dp", split_axis=0, concat_axis=0, tiled=True),
    )
    cache_in = cache_in.reshape((-1,) + cache_in.shape[2:])
    cache_two = jnp.where(incoming[:, None, None], cache_in[source_item], cache_now)
    counts_in = count_in.reshape(-1).astype(jnp.int32)
    counts_two = jnp.where(incoming, counts_in[source_item], jnp.where(vacated, 0, counts_one))
    rows_two = jnp.where(
        incoming[:, None], rows_in.reshape(-1, model_width)[source_item], kept_rows
    )
    second_att, unused_cache = decode_pass(cache_two, queries[1], newest_kv[1], counts_two)
    final_rows = routed_layer(
        rows_two, route_ids[1, 0], route_gates[1, 0], gate_local, up_local, down_local
    )
    return (jnp.stack([first_att, second_att]), final_rows)


def solution(mesh):
    return jax.shard_map(
        body,
        mesh=mesh,
        in_specs=(
            P(("dp", "ep")),
            P(("dp", "ep"), None, None),
            P(("dp", "ep"), None, None),
            P(("dp", "ep"), None, None),
            P(None, ("dp", "ep"), None, None),
            P(None, ("dp", "ep"), None),
            P(("dp", "ep"), None),
            P(None, "ep", None, None),
            P(None, "ep", None, None),
            P("ep", None, "dp"),
            P("ep", None, "dp"),
            P("ep", "dp", None),
        ),
        out_specs=(P(None, ("dp", "ep"), None, None), P(("dp", "ep"), None)),
        check_vma=False,
    )
```

profile of v0, /device:TPU:32, one launch (start us, length us, event | category | flops | bytes accessed | tf_op | source)
XLA Modules:
  0.0 881.6 jit_solution(1690428883188892545)
XLA Ops:
  5.3 16.6 %all-gather = bf16[4,6,7168]{2,1,0:T(8,128)(2,1)S(1)} all-gather(bf16[1,6,7168]{2,1,0:T(8,128)(2,1)S(1)} %fusion.98), channel_id=1, replica_groups=mesh['dp'=4,'ep'=64] {'dp'}, dimensions={0}, use_global_device_ids=true | all-gather | bytes 430080 | tf_op jit(solution)/shard_map/all_gather | solution.py:82
  22.0 4.7 fusion.4
  26.7 167.6 %all_to_all.36 = bf16[64,8,7168]{2,1,0:T(8,128)(2,1)S(1)} all-to-all(bf16[64,8,7168]{2,1,0:T(8,128)(2,1)} %fusion.4), channel_id=1, replica_groups=mesh['dp'=4,'ep'=64] {'ep'}, dimensions={0} | all-to-all | bytes 14680064 | tf_op jit(solution)/shard_map/all_to_all | solution.py:86
  199.4 16.0 %fusion.5 = bf16[64,8,7168]{2,1,0:T(8,128)(2,1)} fusion(bf16[1,256,7168]{2,1,0:T(8,128)(2,1)} %param.23, bf16[1,7168,256]{2,1,0:T(8,128)(2,1)} %param.22, bf16[64,8,7168]{2,1,0:T(8,128)(2,1)} %copy-done, f32[512,256]{1,0:T(8,128)S(1)} %fusion.16), kind=kOutput, calls=%fused_computation.13 | convolution fusion | flops 3762552832 | bytes 22544384 | tf_op jit(solution)/shard_map/dot_general | solution.py:45
  215.4 8.9 %all-to-all-start.3 = ((bf16[64,8,7168]{2,1,0:T(8,128)(2,1)}), bf16[64,8,7168]{2,1,0:T(8,128)(2,1)}, u32[]{:S(2)}, u32[]{:S(2)}) async-start(bf16[64,8,7168]{2,1,0:T(8,128)(2,1)} %fusion.5), calls=%async_computation.3 | async-start | bytes 14680064 | tf_op jit(solution)/shard_map/all_to_all | solution.py:88
  228.3 115.8 %all-to-all-done.3 = bf16[64,8,7168]{2,1,0:T(8,128)(2,1)} async-done(((bf16[64,8,7168]{2,1,0:T(8,128)(2,1)}), bf16[64,8,7168]{2,1,0:T(8,128)(2,1)}, u32[]{:S(2)}, u32[]{:S(2)}) %all-to-all-start.3) | async-done | bytes 7340064 | tf_op jit(solution)/shard_map/all_to_all | solution.py:88
  344.0 5.2 convolution_convert_fusion.5
  349.2 65.9 %fusion = bf16[8,7168]{1,0:T(8,128)(2,1)S(1)} fusion(bf16[24,7168]{1,0:T(8,128)(2,1)S(1)} %convolution_convert_fusion.5), kind=kCustom, calls=%all-reduce-scatter | all-reduce-scatter fusion | flops 229377 | bytes 459776
  417.6 4.5 collective-permute-done
  425.1 3.9 all-to-all-start.4
  429.1 4.6 all-to-all-done.4
  433.6 4.3 all-to-all-start
  439.0 15.4 %all-gather.1 = bf16[4,6,7168]{2,1,0:T(8,128)(2,1)S(1)} all-gather(bf16[1,6,7168]{2,1,0:T(8,128)(2,1)S(1)} %fusion.97), channel_id=1, replica_groups=mesh['dp'=4,'ep'=64] {'dp'}, dimensions={0}, use_global_device_ids=true | all-gather | bytes 430080 | tf_op jit(solution)/shard_map/all_gather | solution.py:82
  454.6 4.8 fusion.6
  459.4 9.4 %all-to-all-start.5 = ((bf16[64,8,7168]{2,1,0:T(8,128)(2,1)}), bf16[64,8,7168]{2,1,0:T(8,128)(2,1)}, u32[]{:S(2)}, u32[]{:S(2)}) async-start(bf16[64,8,7168]{2,1,0:T(8,128)(2,1)} %fusion.6), calls=%async_computation.5 | async-start | bytes 14680064 | tf_op jit(solution)/shard_map/all_to_all | solution.py:86
  471.4 126.8 %all-to-all-done.5 = bf16[64,8,7168]{2,1,0:T(8,128)(2,1)} async-done(((bf16[64,8,7168]{2,1,0:T(8,128)(2,1)}), bf16[64,8,7168]{2,1,0:T(8,128)(2,1)}, u32[]{:S(2)}, u32[]{:S(2)}) %all-to-all-start.5) | async-done | bytes 7340064 | tf_op jit(solution)/shard_map/all_to_all | solution.py:86
  598.2 49.5 %all-to-all-start.1 = ((bf16[4,1,64,576]{3,2,1,0:T(8,128)(2,1)}), bf16[4,1,64,576]{3,2,1,0:T(8,128)(2,1)S(1)}, u32[]{:S(2)}, u32[]{:S(2)}) async-start(bf16[4,1,64,576]{3,2,1,0:T(8,128)(2,1)} %fusion.82), calls=%async_computation.1 | async-start | bytes 655360 | tf_op jit(solution)/shard_map/all_to_all | solution.py:141
  647.7 6.2 fusion.11
  653.9 16.0 %fusion.7 = bf16[64,8,7168]{2,1,0:T(8,128)(2,1)} fusion(bf16[1,256,7168]{2,1,0:T(8,128)(2,1)} %param.23, bf16[1,7168,256]{2,1,0:T(8,128)(2,1)} %param.22, bf16[64,8,7168]{2,1,0:T(8,128)(2,1)} %all-to-all-done.5, f32[512,256]{1,0:T(8,128)S(1)} %fusion.11), kind=kOutput, calls=%fused_computation.15 | convolution fusion | flops 3762552832 | bytes 22544384 | tf_op jit(solution)/shard_map/dot_general | solution.py:45
  669.9 5.8 all-to-all-start.6
  678.9 137.8 %all-to-all-done.6 = bf16[64,8,7168]{2,1,0:T(8,128)(2,1)} async-done(((bf16[64,8,7168]{2,1,0:T(8,128)(2,1)}), bf16[64,8,7168]{2,1,0:T(8,128)(2,1)}, u32[]{:S(2)}, u32[]{:S(2)}) %all-to-all-start.6) | async-done | bytes 7340064 | tf_op jit(solution)/shard_map/all_to_all | solution.py:88
  816.6 5.2 convolution_convert_fusion.4
  821.8 50.3 %fusion.1 = bf16[8,7168]{1,0:T(8,128)(2,1)S(1)} fusion(bf16[24,7168]{1,0:T(8,128)(2,1)S(1)} %convolution_convert_fusion.4), kind=kCustom, calls=%all-reduce-scatter.1 | all-reduce-scatter fusion | flops 229377 | bytes 459776
  872.1 3.8 collective-permute-start.1
  (118 shorter events, 30.9 us)
Async XLA Ops:
  26.7 170.6 %copy-start.9 = (bf16[1,7168,256]{2,1,0:T(8,128)(2,1)S(1)}, bf16[1,7168,256]{2,1,0:T(8,128)(2,1)}, u32[]{:S(2)}) copy-start(bf16[1,7168,256]{2,1,0:T(8,128)(2,1)} %param.21) | copy-start | bytes 11010052
  194.3 3.0 copy-start
  215.4 8.9 %copy-start.4 = (s32[2,1,24,8]{2,3,1,0:T(8,128)S(1)}, s32[2,1,24,8]{2,3,1,0:T(8,128)}, u32[]{:S(2)}) copy-start(s32[2,1,24,8]{2,3,1,0:T(8,128)} %param.20) | copy-start | bytes 4612
  215.4 9.3 %copy-start.7 = (s32[1,4,1]{1,2,0:T(1,128)S(1)}, s32[1,4,1]{1,2,0:T(1,128)}, u32[]{:S(2)}) copy-start(s32[1,4,1]{1,2,0:T(1,128)} %param.13) | copy-start | bytes 52
  215.4 9.3 %copy-start.5 = (s32[6]{0:T(128)S(1)}, s32[6]{0:T(128)}, u32[]{:S(2)}) copy-start(s32[6]{0:T(128)} %param.12) | copy-start | bytes 76
  215.4 10.7 %copy-start.8 = (u32[256]{0:T(256)S(1)}, u32[256]{0:T(256)}, u32[]{:S(2)}) copy-start(u32[256]{0:T(256)} %constant.90) | copy-start | bytes 3076
  215.4 11.9 %copy-start.6 = (s32[1,4,1]{1,2,0:T(1,128)S(1)}, s32[1,4,1]{1,2,0:T(1,128)}, u32[]{:S(2)}) copy-start(s32[1,4,1]{1,2,0:T(1,128)} %param.14) | copy-start | bytes 52
  215.4 128.6 %all-to-all-start.3 = ((bf16[64,8,7168]{2,1,0:T(8,128)(2,1)}), bf16[64,8,7168]{2,1,0:T(8,128)(2,1)}, u32[]{:S(2)}, u32[]{:S(2)}) async-start(bf16[64,8,7168]{2,1,0:T(8,128)(2,1)} %fusion.5), calls=%async_computation.3 | async-start | bytes 14680064 | tf_op jit(solution)/shard_map/all_to_all | solution.py:88
  224.3 198.2 %copy-start.2 = (bf16[6,7168]{1,0:T(8,128)(2,1)S(1)}, bf16[6,7168]{1,0:T(8,128)(2,1)}, u32[]{:S(2)}) copy-start(bf16[6,7168]{1,0:T(8,128)(2,1)} %param.18) | copy-start | bytes 258052
  415.1 7.0 collective-permute-start
  425.1 8.5 all-to-all-start.4
  433.6 25.8 %all-to-all-start = ((bf16[4,1,1]{2,1,0:T(2,128)(2,1)}), bf16[4,1,1]{2,1,0:T(2,128)(2,1)S(1)}, u32[]{:S(2)}, u32[]{:S(2)}) async-start(bf16[4,1,1]{2,1,0:T(2,128)(2,1)} %copy.54), calls=%async_computation | async-start | bytes 4096 | tf_op jit(solution)/shard_map/all_to_all | solution.py:143
  459.4 9.4 %copy-start.3 = (bf16[2,6,576]{2,0,1:T(2,128)(2,1)S(1)}, bf16[2,6,576]{2,0,1:T(2,128)(2,1)}, u32[]{:S(2)}) copy-start(bf16[2,6,576]{2,0,1:T(2,128)(2,1)} %param.17) | copy-start | bytes 41476
  459.4 10.4 %copy-start.1 = (bf16[6,64,576]{2,1,0:T(8,128)(2,1)S(1)}, bf16[6,64,576]{2,1,0:T(8,128)(2,1)}, u32[]{:S(2)}) copy-start(bf16[6,64,576]{2,1,0:T(8,128)(2,1)} %param.15) | copy-start | bytes 1327108
  459.4 138.8 %all-to-all-start.5 = ((bf16[64,8,7168]{2,1,0:T(8,128)(2,1)}), bf16[64,8,7168]{2,1,0:T(8,128)(2,1)}, u32[]{:S(2)}, u32[]{:S(2)}) async-start(bf16[64,8,7168]{2,1,0:T(8,128)(2,1)} %fusion.6), calls=%async_computation.5 | async-start | bytes 14680064 | tf_op jit(solution)/shard_map/all_to_all | solution.py:86
  598.2 71.7 %all-to-all-start.1 = ((bf16[4,1,64,576]{3,2,1,0:T(8,128)(2,1)}), bf16[4,1,64,576]{3,2,1,0:T(8,128)(2,1)S(1)}, u32[]{:S(2)}, u32[]{:S(2)}) async-start(bf16[4,1,64,576]{3,2,1,0:T(8,128)(2,1)} %fusion.82), calls=%async_computation.1 | async-start | bytes 655360 | tf_op jit(solution)/shard_map/all_to_all | solution.py:141
  669.9 6.5 copy-start.10
  669.9 146.7 %all-to-all-start.6 = ((bf16[64,8,7168]{2,1,0:T(8,128)(2,1)}), bf16[64,8,7168]{2,1,0:T(8,128)(2,1)}, u32[]{:S(2)}, u32[]{:S(2)}) async-start(bf16[64,8,7168]{2,1,0:T(8,128)(2,1)} %fusion.7), calls=%async_computation.6 | async-start | bytes 14680064 | tf_op jit(solution)/shard_map/all_to_all | solution.py:88
  872.1 8.4 collective-permute-start.1
where the time goes:
time: 882 us
  waiting for transfers between devices  393 us (45%)
  blocking collectives  316 us (36%)
  starting transfers between devices  88.2 us (10%)
  matrix products  61.9 us (7%)
  local copies, waits for them, and re-layouts  12 us (1%)
  other arithmetic  8.91 us (1%)
    all_to_all x2, waiting for transfers between devices, routed_layer(): lax.all_to_all(partial_value.reshape(received.shape), 'ep', split_axis=0,...  254 us
    all_to_all x1, blocking collectives, routed_layer(): lax.all_to_all(outgoing, 'ep', split_axis=0, concat_axis=0, tiled=True)  168 us
    all_to_all x1, waiting for transfers between devices, routed_layer(): lax.all_to_all(outgoing, 'ep', split_axis=0, concat_axis=0, tiled=True)  127 us
    unnamed x2, blocking collectives  116 us
    all_to_all x1, starting transfers between devices, body(): lax.all_to_all(cache_out, 'dp', split_axis=0, concat_axis=0, tiled=True)  49.5 us
    all_gather x2, blocking collectives, routed_layer(): column = lax.all_gather(normed, 'dp', axis=0, tiled=True)  32.1 us
    dot_general x2, matrix products, expert_rows(): jnp.dot(inner_rows, down_local, preferred_element_type=jnp.float32)  32 us
  transfers between devices with their start and end apart: 8, of which 6 were waited for; matrix products, arithmetic and copies ran while one was open for 4% of the time, Pallas kernels for 0%

commit v1 on v0

v1 whole, which is shorter than its diff:
```python
import jax
import jax.numpy as jnp
from jax import lax
from jax.experimental import pallas as pl
from jax.experimental.pallas import tpu as pltpu
from jax.sharding import PartitionSpec as P

LAT = 512
WIDTH = 7168
GATE_COLS = 128
PAYLOAD = WIDTH + GATE_COLS
EXPERTS = 64
CHUNK = 1792
VMEM_LIMIT = 44 * 1024 * 1024
AXES = ("dp", "ep")
SIZES = {"x": 4, "y": 4, "z": 8}

softmax_scale = 192.0 ** (-0.5)
route_scale = 2.5
norm_eps = 1e-06


def device_index(x, y, z, core):
    return (z % 4) * 64 + ((x * 4 + y) * 2 + z // 4) * 2 + core


def every_device():
    return [
        (x, y, z, core)
        for x in range(SIZES["x"])
        for y in range(SIZES["y"])
        for z in range(SIZES["z"])
        for core in range(2)
    ]


def swap(value):
    pairs = [
        (device_index(x, y, z, core), device_index(x, y, z, 1 - core))
        for x, y, z, core in every_device()
    ]
    return lax.ppermute(value, AXES, pairs)


def shift(value, axis, distance):
    pairs = []
    for x, y, z, core in every_device():
        step = distance if core == 0 else -distance
        place = {"x": x, "y": y, "z": z}
        place[axis] = (place[axis] + step) % SIZES[axis]
        pairs.append(
            (device_index(x, y, z, core), device_index(place["x"], place["y"], place["z"], core))
        )
    return lax.ppermute(value, AXES, pairs)


def total(*values):
    result = values[0].astype(jnp.float32)
    for value in values[1:]:
        result = result + value.astype(jnp.float32)
    return result


def rounded(*values):
    return total(*values).astype(jnp.bfloat16)


def tied(values, others):
    held = lax.optimization_barrier((tuple(values), tuple(others)))
    return list(held[0]), list(held[1])


def expert_kernel(block_rows, steps, expert_ref, *refs):
    count = len(block_rows)
    rows_refs, route_refs = refs[:count], refs[count : 2 * count]
    gate_refs, up_refs, down_refs = (
        refs[2 * count : 2 * count + 2],
        refs[2 * count + 2 : 2 * count + 4],
        refs[2 * count + 4 : 2 * count + 6],
    )
    out_refs = refs[2 * count + 6 : 3 * count + 6]
    rows_all, gate_sum, up_sum, inner = refs[3 * count + 6 :]
    step = pl.program_id(0)

    @pl.when(step < steps)
    def _():
        start = 0
        for ref, size in zip(rows_refs, block_rows):
            rows_all[start : start + size, :] = ref[...]
            start += size
        rows_now = rows_all[...]
        gate_part = [
            jnp.dot(rows_now, ref[...], preferred_element_type=jnp.float32) for ref in gate_refs
        ]
        up_part = [
            jnp.dot(rows_now, ref[...], preferred_element_type=jnp.float32) for ref in up_refs
        ]

        @pl.when(step == 0)
        def _():
            for k in range(2):
                gate_sum[k] = gate_part[k]
                up_sum[k] = up_part[k]

        @pl.when(step > 0)
        def _():
            for k in range(2):
                gate_sum[k] += gate_part[k]
                up_sum[k] += up_part[k]

    @pl.when(step == steps - 1)
    def _():
        start = 0
        for ref, size in zip(route_refs, block_rows):
            routes = ref[...].astype(jnp.float32)
            column = lax.broadcasted_iota(jnp.int32, routes.shape, 1)
            whole = jnp.sum(jnp.where(column == EXPERTS, routes, 0.0), axis=1, keepdims=True)
            for k in range(2):
                mine = jnp.sum(
                    jnp.where(column == expert_ref[k], routes, 0.0), axis=1, keepdims=True
                )
                weight = route_scale * mine / whole
                gate_val = gate_sum[k, start : start + size, :]
                units = gate_val * jax.nn.sigmoid(gate_val) * up_sum[k, start : start + size, :]
                inner[k, start : start + size, :] = (units * weight).astype(jnp.bfloat16)
            start += size

    @pl.when(step >= steps)
    def _():
        result = jnp.dot(inner[0], down_refs[0][...], preferred_element_type=jnp.float32)
        result += jnp.dot(inner[1], down_refs[1][...], preferred_element_type=jnp.float32)
        result = result.astype(jnp.bfloat16)
        start = 0
        for ref, size in zip(out_refs, block_rows):
            ref[...] = result[start : start + size, :]
            start += size


def expert_call(blocks, expert, weights):
    block_rows = [block.shape[0] for block in blocks]
    rows = sum(block_rows)
    width = weights[0].shape[1]
    units = weights[0].shape[2]
    steps = width // CHUNK
    last = steps - 1

    def first_phase(k, expert_ref):
        return (0, jnp.minimum(k, last))

    def weight_in(k, expert_ref):
        return (0, jnp.minimum(k, last), 0)

    def weight_out(k, expert_ref):
        return (0, 0, jnp.maximum(k - steps, 0))

    def second_phase(k, expert_ref):
        return (0, jnp.maximum(k - steps, 0))

    def body(expert_ref, *refs):
        expert_kernel(block_rows, steps, expert_ref, *refs)

    return pl.pallas_call(
        body,
        grid_spec=pltpu.PrefetchScalarGridSpec(
            num_scalar_prefetch=1,
            grid=(2 * steps,),
            in_specs=[pl.BlockSpec((size, CHUNK), first_phase) for size in block_rows]
            + [
                pl.BlockSpec((size, GATE_COLS), lambda k, e: (0, WIDTH // GATE_COLS))
                for size in block_rows
            ]
            + [pl.BlockSpec((None, CHUNK, units), weight_in)] * 4
            + [pl.BlockSpec((None, units, CHUNK), weight_out)] * 2,
            out_specs=[pl.BlockSpec((size, CHUNK), second_phase) for size in block_rows],
            scratch_shapes=[
                pltpu.VMEM((rows, CHUNK), jnp.bfloat16),
                pltpu.VMEM((2, rows, units), jnp.float32),
                pltpu.VMEM((2, rows, units), jnp.float32),
                pltpu.VMEM((2, rows, units), jnp.bfloat16),
            ],
        ),
        out_shape=[jax.ShapeDtypeStruct((size, width), jnp.bfloat16) for size in block_rows],
        compiler_params=pltpu.CompilerParams(vmem_limit_bytes=VMEM_LIMIT),
        cost_estimate=pl.CostEstimate(
            flops=2 * rows * width * units * 6,
            bytes_accessed=6 * width * units * 2 + 2 * rows * width * 2,
            transcendentals=2 * rows * units,
        ),
    )(expert, *blocks, *blocks, *weights)


def normed_rows(hidden):
    values = hidden.astype(jnp.float32)
    inverse = lax.rsqrt(jnp.mean(values * values, axis=1, keepdims=True) + norm_eps)
    return (values * inverse).astype(jnp.bfloat16)


def decode_pass(cache_rows, queries_now, newest, counts):
    positions = lax.broadcasted_iota(jnp.int32, cache_rows.shape[:2], 1)
    is_live = counts > 0
    placed = (positions == counts[:, None]) & is_live[:, None]
    cache_rows = jnp.where(placed[:, :, None], newest[:, None, :], cache_rows)
    scores = (
        jnp.einsum("nhk,ntk->nht", queries_now, cache_rows, preferred_element_type=jnp.float32)
        * softmax_scale
    )
    usable = positions <= counts[:, None]
    scores = jnp.where(usable[:, None, :], scores, -1e30)
    peak_score = jnp.max(scores, axis=2, keepdims=True)
    raised = jnp.exp(scores - peak_score)
    chances = (raised / jnp.sum(raised, axis=2, keepdims=True)).astype(jnp.bfloat16)
    output = jnp.einsum(
        "nht,ntl->nhl", chances, cache_rows[:, :, :LAT], preferred_element_type=jnp.float32
    )
    output = jnp.where(is_live[:, None, None], output, 0.0).astype(jnp.bfloat16)
    return (output, cache_rows)


def route_columns(column_ids, column_gates, slot_count):
    first = lax.axis_index("dp") * slot_count
    ids = lax.dynamic_slice_in_dim(column_ids, first, slot_count, axis=0)
    gates = lax.dynamic_slice_in_dim(column_gates, first, slot_count, axis=0)
    column = lax.broadcasted_iota(jnp.int32, (1, 1, GATE_COLS), 2)
    spread = jnp.sum(jnp.where(ids[:, :, None] == column, gates[:, :, None], 0), axis=1)
    whole = jnp.sum(gates, axis=1, keepdims=True)
    column = lax.broadcasted_iota(jnp.int32, (1, GATE_COLS), 1)
    return jnp.where(column == EXPERTS, whole, spread).astype(jnp.bfloat16)


def send_direct(half, other, axis):
    reach = SIZES[axis] // 2
    both = jnp.concatenate([half, other], axis=0)
    return [shift(both, axis, k) for k in range(1, reach)] + [shift(half, axis, reach)]


def return_direct(sums, axis):
    reach = SIZES[axis] // 2
    rows = sums.shape[0] // SIZES[axis]
    arrived = [
        shift(sums[rows * (2 * k - 1) : rows * (2 * k + 1)], axis, -k) for k in range(1, reach)
    ]
    far = shift(sums[rows * (2 * reach - 1) :], axis, -reach)
    first = total(sums[:rows], far, *[piece[:rows] for piece in arrived])
    second = rounded(*[piece[rows:] for piece in arrived])
    return first, second


def routed_layer(hidden, routes, expert, weights):
    payload = jnp.concatenate([normed_rows(hidden), routes], axis=1)

    def experts(blocks):
        return expert_call(blocks, expert, weights)

    other = swap(payload)
    got = send_direct(payload[:4], other[:4], "z")
    got_z = send_direct(payload[4:], other[4:], "x")
    flat = jnp.concatenate([payload[4:], *got_z], axis=0)
    got_z = send_direct(flat, swap(flat), "y")
    z_half = jnp.concatenate([flat, *got_z], axis=0)
    column = jnp.concatenate([payload[:4], *got], axis=0)
    z_both = jnp.concatenate([z_half, swap(z_half)], axis=0)
    (z_both,), (column,) = tied([z_both], [column])
    z_near = shift(z_both, "z", 1)
    column = column.reshape(-1, 2, 2 * PAYLOAD)
    x_col = column[:, 0].reshape(-1, PAYLOAD)
    y_col = column[:, 1].reshape(-1, PAYLOAD)
    x_got = send_direct(x_col, swap(x_col), "y")
    y_got = send_direct(y_col, swap(y_col), "x")
    x_f = jnp.concatenate([x_col, *x_got], axis=0)
    y_f = jnp.concatenate([y_col, *y_got], axis=0)

    (x_f, y_f, z_near), _ = tied([x_f, y_f, z_near], [])
    x_g, y_g = swap(x_f), swap(y_f)
    x1f, y1f, z_mid = shift(x_f, "x", 1), shift(y_f, "y", 1), shift(z_near, "z", 1)
    first = experts([x_f, y_f, z_half, z_near])

    (x_g, y_g, z_mid), (x1f, y1f, *first) = tied([x_g, y_g, z_mid], [x1f, y1f, *first])
    x1g, y1g, z_far = shift(x_g, "x", 1), shift(y_g, "y", 1), shift(z_mid, "z", 1)
    second = experts([x1f, y1f, z_mid])

    (x1f_on, y1f_on, z_far), (x1g, y1g, *second) = tied([x1f, y1f, z_far], [x1g, y1g, *second])
    x2, y2 = shift(x1f_on, "x", 1), shift(y1f_on, "y", 1)
    z_end = shift(z_far[: z_far.shape[0] // 2], "z", 1)
    third = experts([x1g, y1g, z_far])
    (x2, y2, z_end), third = tied([x2, y2, z_end], third)
    last = experts([x2, y2, z_end])

    ox_f, oy_f, oz_half, tz_near = first
    tx1f, ty1f, tz_mid = second
    tx1g, ty1g, tz_far = third
    (tx2, ty2, tz_end), _ = tied(last, [])
    bx2, by2, bz_end = shift(tx2, "x", -1), shift(ty2, "y", -1), shift(tz_end, "z", -1)

    half = tz_end.shape[0]
    tx1f, ty1f = rounded(tx1f, bx2), rounded(ty1f, by2)
    tz_far = jnp.concatenate([rounded(tz_far[:half], bz_end), tz_far[half:]], axis=0)
    (tx1f, ty1f, tz_far), _ = tied([tx1f, ty1f, tz_far], [])
    bx1f, by1f, bz_far = shift(tx1f, "x", -1), shift(ty1f, "y", -1), shift(tz_far, "z", -1)

    tz_mid = rounded(tz_mid, bz_far)
    (tx1g, ty1g, tz_mid), (bx1f, by1f) = tied([tx1g, ty1g, tz_mid], [bx1f, by1f])
    bx1g, by1g, bz_mid = shift(tx1g, "x", -1), shift(ty1g, "y", -1), shift(tz_mid, "z", -1)

    tz_near = rounded(tz_near, bz_mid)
    (tz_near,), (bx1g, by1g) = tied([tz_near], [bx1g, by1g])
    bz_near = shift(tz_near, "z", -1)
    x_sum = rounded(ox_f, bx1f, swap(bx1g))
    y_sum = rounded(oy_f, by1f, swap(by1g))
    x_first, x_second = return_direct(x_sum, "y")
    y_first, y_second = return_direct(y_sum, "x")
    x_col = rounded(x_first, swap(x_second))
    y_col = rounded(y_first, swap(y_second))
    column = jnp.concatenate(
        [x_col.reshape(-1, 1, 2 * WIDTH), y_col.reshape(-1, 1, 2 * WIDTH)], axis=1
    ).reshape(-1, WIDTH)
    z_sum = rounded(oz_half, bz_near[:half], swap(bz_near[half:]))
    (column, z_sum), _ = tied([column, z_sum], [])
    first, second = return_direct(column, "z")
    z_first, z_second = return_direct(z_sum, "y")
    z_first, z_second = return_direct(rounded(z_first, swap(z_second)), "x")
    other = swap(jnp.concatenate([second, z_second], axis=0))
    addition = total(jnp.concatenate([first, z_first], axis=0), other)
    return (hidden.astype(jnp.float32) + addition).astype(jnp.bfloat16)


def from_peers(value):
    ranks = lax.axis_size("dp")
    return [
        lax.ppermute(value, "dp", [(i, (i + k) % ranks) for i in range(ranks)])
        for k in range(1, ranks)
    ]


def body(
    lengths,
    send_slots,
    recv_slots,
    latent_cache,
    queries,
    newest_kv,
    hidden_rows,
    route_ids,
    route_gates,
    w_gate,
    w_up,
    w_down,
):
    slot_count = lengths.shape[0]
    ranks = lax.axis_size("dp")
    rank = lax.axis_index("dp")
    expert = lax.axis_index("ep").astype(jnp.int32)
    expert = jnp.stack([expert, expert + 1 - 2 * (expert % 2)])
    local_slots = jnp.arange(slot_count, dtype=jnp.int32)
    leaving = jnp.min(send_slots)
    vacated = local_slots == leaving
    chosen = jnp.minimum(leaving, slot_count - 1)
    landings = [
        local_slots == lax.dynamic_index_in_dim(recv_slots[0, :, 0], (rank - k) % ranks, 0, False)
        for k in range(1, ranks)
    ]

    weights = [w_gate, swap(w_gate)]
    (later,), (weights[1],) = tied([w_up], [weights[1]])
    weights += [w_up, swap(later)]
    (later,), (weights[3],) = tied([w_down], [weights[3]])
    weights += [w_down, swap(later)]

    rows_one = routed_layer(
        hidden_rows,
        route_columns(route_ids[0, 0], route_gates[0, 0], slot_count),
        expert,
        weights,
    )

    first_att, cache_now = decode_pass(latent_cache, queries[0], newest_kv[0], lengths)
    counts_one = jnp.where(lengths > 0, lengths + 1, 0)
    cache_out = lax.dynamic_index_in_dim(cache_now, chosen, 0, False)
    count_out = lax.dynamic_index_in_dim(counts_one, chosen, 0, True).astype(jnp.bfloat16)
    moving = jnp.concatenate(
        [cache_out, jnp.broadcast_to(count_out, (8, cache_out.shape[1]))], axis=0
    )
    cap = cache_out.shape[0]
    cache_two = cache_now
    counts_two = jnp.where(vacated, 0, counts_one)
    for landing, arrived in zip(landings, from_peers(moving)):
        cache_two = jnp.where(landing[:, None, None], arrived[None, :cap], cache_two)
        counts_two = jnp.where(landing, arrived[cap, 0].astype(jnp.int32), counts_two)
    second_att, unused_cache = decode_pass(cache_two, queries[1], newest_kv[1], counts_two)

    row_out = lax.dynamic_index_in_dim(rows_one, chosen, 0, True)
    rows_two = jnp.where(vacated[:, None], jnp.zeros_like(rows_one), rows_one)
    for landing, row_in in zip(landings, from_peers(row_out)):
        rows_two = jnp.where(landing[:, None], row_in, rows_two)
    final_rows = routed_layer(
        rows_two,
        route_columns(route_ids[1, 0], route_gates[1, 0], slot_count),
        expert,
        weights,
    )
    return (jnp.stack([first_att, second_att]), final_rows)


def solution(mesh):
    return jax.shard_map(
        body,
        mesh=mesh,
        in_specs=(
            P(("dp", "ep")),
            P(("dp", "ep"), None, None),
            P(("dp", "ep"), None, None),
            P(("dp", "ep"), None, None),
            P(None, ("dp", "ep"), None, None),
            P(None, ("dp", "ep"), None),
            P(("dp", "ep"), None),
            P(None, "ep", None, None),
            P(None, "ep", None, None),
            P("ep", None, "dp"),
            P("ep", None, "dp"),
            P("ep", "dp", None),
        ),
        out_specs=(P(None, ("dp", "ep"), None, None), P(("dp", "ep"), None)),
        check_vma=False,
    )
```

time: 882 us -> 525 us (0.60)
  blocking collectives: 316 us -> 0 us
  waiting for transfers between devices: 393 us -> 176 us
  Pallas kernels: 0 us -> 103 us
  starting transfers between devices: 88.2 us -> 162 us
  matrix products: 61.9 us -> 4.23 us
  local copies, waits for them, and re-layouts: 12 us -> 40.5 us
  other arithmetic: 8.91 us -> 24.8 us
    all_to_all x6 -> x0, waiting for transfers between devices: 385 us -> none  [the longest x2 254 us: routed_layer(): lax.all_to_all(partial_value.reshape(received.shape), 'ep', split_axis=0,...]
    ppermute x0 -> x125, waiting for transfers between devices: none -> 176 us  [the longest x88 171 us: shift(): return lax.ppermute(value, AXES, pairs)]
    all_to_all x1 -> x0, blocking collectives: 168 us -> none  [routed_layer(): lax.all_to_all(outgoing, 'ep', split_axis=0, concat_axis=0, tiled=True)]
    ppermute x0 -> x125, starting transfers between devices: none -> 162 us  [the longest x88 146 us: shift(): return lax.ppermute(value, AXES, pairs)]
    unnamed x2 -> x0, blocking collectives: 116 us -> none
    pallas_call x0 -> x8, Pallas kernels: none -> 103 us  [expert_call(): pl.pallas_call(body, grid_spec=pltpu.PrefetchScalarGridSpec(num_scalar_pr...]
    all_to_all x6 -> x0, starting transfers between devices: 82 us -> none  [the longest x1 49.5 us: body(): lax.all_to_all(cache_out, 'dp', split_axis=0, concat_axis=0, tiled=True)]
    dot_general x10 -> x0, matrix products: 60.6 us -> none  [the longest x2 32 us: expert_rows(): jnp.dot(inner_rows, down_local, preferred_element_type=jnp.float32)]
  transfers between devices with their start and end apart: 8 -> 125, of which waited for: 6 -> 52; matrix products, arithmetic and copies ran while one was open for 4% -> 10% of each run, Pallas kernels for 0% -> 15%
where the time goes in v1:
time: 525 us; the launch traced here: 516 us
  waiting for transfers between devices  176 us (34%)
  starting transfers between devices  162 us (31%)
  Pallas kernels  103 us (20%)
  local copies, waits for them, and re-layouts  40.5 us (8%)
  other arithmetic  24.8 us (5%)
  between operations  5.86 us (1%)
    ppermute x88, waiting for transfers between devices, shift(): return lax.ppermute(value, AXES, pairs)  171 us
    ppermute x88, starting transfers between devices, shift(): return lax.ppermute(value, AXES, pairs)  146 us
    pallas_call x8, Pallas kernels, expert_call(): pl.pallas_call(body, grid_spec=pltpu.PrefetchScalarGridSpec(num_scalar_pr...  103 us
  transfers between devices with their start and end apart: 125, of which 52 were waited for; matrix products, arithmetic and copies ran while one was open for 10% of the time, Pallas kernels for 15%

profile of v1, /device:TPU:32, one launch (start us, length us, event | category | flops | bytes accessed | tf_op | source)
XLA Modules:
  0.0 516.1 jit_solution(18328608198774269422)
XLA Ops:
  20.1 6.4 %collective-permute-start.13 = (bf16[4,7296]{1,0:T(4,128)(2,1)S(1)}, bf16[4,7296]{1,0:T(4,128)(2,1)S(1)}, u32[]{:S(2)}, u32[]{:S(2)}) collective-permute-start(bf16[4,7296]{1,0:T(4,128)(2,1)S(1)} %fusion.29), channel_id=1, source_target_pairs={{0,2},{1,3},{64,66},{65,67},{128,130},{129,131},{192,194},{193,195... | collective-permute-start | bytes 175112 | tf_op jit(solution)/shard_map/ppermute | solution.py:54
  36.0 6.6 %collective-permute-done.12 = bf16[8,7296]{1,0:T(8,128)(2,1)S(1)} collective-permute-done((bf16[8,7296]{1,0:T(8,128)(2,1)S(1)}, bf16[8,7296]{1,0:T(8,128)(2,1)S(1)}, u32[]{:S(2)}, u32[]{:S(2)}) %collective-permute-start.12) | collective-permute-done | bytes 116768 | tf_op jit(solution)/shard_map/ppermute | solution.py:54
  63.6 6.8 %collective-permute-done.18 = bf16[32,7296]{1,0:T(8,128)(2,1)S(1)} collective-permute-done((bf16[32,7296]{1,0:T(8,128)(2,1)S(1)}, bf16[32,7296]{1,0:T(8,128)(2,1)S(1)}, u32[]{:S(2)}, u32[]{:S(2)}) %collective-permute-start.18) | collective-permute-done | bytes 466976 | tf_op jit(solution)/shard_map/ppermute | solution.py:54
  78.7 13.5 %shard_map.131 = (bf16[64,7168]{1,0:T(8,128)(2,1)S(1)}, bf16[64,7168]{1,0:T(8,128)(2,1)S(1)}, bf16[32,7168]{1,0:T(8,128)(2,1)S(1)}, bf16[64,7168]{1,0:T(8,128)(2,1)S(1)}) custom-call(s32[2]{0:T(128)S(1)} %pad_add_fusion.expert_ref, bf16[64,7296]{1,0:T(8,128)(2,1)S(1)} %pad_maximum_fusion.refs_0_.refs_4_, ...), custom_call_target="tpu_custom_call" | custom-call | flops 4932501504 | bytes 28442624 | tf_op jit(solution)/shard_map/pallas_call | solution.py:162
  96.9 13.1 %shard_map.132 = (bf16[64,7168]{1,0:T(8,128)(2,1)S(1)}, bf16[64,7168]{1,0:T(8,128)(2,1)S(1)}, bf16[64,7168]{1,0:T(8,128)(2,1)S(1)}) custom-call(s32[2]{0:T(128)S(1)} %pad_add_fusion.expert_ref, bf16[64,7296]{1,0:T(8,128)(2,1)S(1)} %collective-permute-done.24.refs_0_.refs_3_, bf16[64,7296]{1,0:T(8,128)(2,1)} %collective-permute-done.25.refs_1_.refs_4_, ...), custom_call_target="tpu_custom_call" | custom-call | flops 4227858432 | bytes 27525120 | tf_op jit(solution)/shard_map/pallas_call | solution.py:162
  114.2 12.7 %shard_map.133 = (bf16[64,7168]{1,0:T(8,128)(2,1)S(1)}, bf16[64,7168]{1,0:T(8,128)(2,1)S(1)}, bf16[64,7168]{1,0:T(8,128)(2,1)S(1)}) custom-call(s32[2]{0:T(128)S(1)} %pad_add_fusion.expert_ref, bf16[64,7296]{1,0:T(8,128)(2,1)S(1)} %collective-permute-done.30.refs_0_.refs_3_, bf16[64,7296]{1,0:T(8,128)(2,1)S(1)} %collective-permute-done.31.refs_1_.refs_4_, ...), custom_call_target="tpu_custom_call" | custom-call | flops 4227858432 | bytes 27525120 | tf_op jit(solution)/shard_map/pallas_call | solution.py:162
  127.1 12.2 %shard_map.134 = (bf16[64,7168]{1,0:T(8,128)(2,1)S(1)}, bf16[64,7168]{1,0:T(8,128)(2,1)S(1)}, bf16[32,7168]{1,0:T(8,128)(2,1)S(1)}) custom-call(s32[2]{0:T(128)S(1)} %pad_add_fusion.expert_ref, bf16[64,7296]{1,0:T(8,128)(2,1)S(1)} %collective-permute-done.32.refs_0_.refs_3_, bf16[64,7296]{1,0:T(8,128)(2,1)S(1)} %collective-permute-done.33.refs_1_.refs_4_, ...), custom_call_target="tpu_custom_call" | custom-call | flops 3523215360 | bytes 26607616 | tf_op jit(solution)/shard_map/pallas_call | solution.py:162
  148.0 7.0 %collective-permute-done.36 = bf16[64,7168]{1,0:T(8,128)(2,1)S(1)} collective-permute-done((bf16[64,7168]{1,0:T(8,128)(2,1)S(1)}, bf16[64,7168]{1,0:T(8,128)(2,1)S(1)}, u32[]{:S(2)}, u32[]{:S(2)}) %collective-permute-start.36) | collective-permute-done | bytes 917536 | tf_op jit(solution)/shard_map/ppermute | solution.py:54
  164.0 6.6 %collective-permute-done.38 = bf16[64,7168]{1,0:T(8,128)(2,1)S(1)} collective-permute-done((bf16[64,7168]{1,0:T(8,128)(2,1)S(1)}, bf16[64,7168]{1,0:T(8,128)(2,1)S(1)}, u32[]{:S(2)}, u32[]{:S(2)}) %collective-permute-start.38) | collective-permute-done | bytes 917536 | tf_op jit(solution)/shard_map/ppermute | solution.py:54
  179.8 10.2 %collective-permute-done.41 = bf16[64,7168]{1,0:T(8,128)(2,1)S(1)} collective-permute-done((bf16[64,7168]{1,0:T(8,128)(2,1)S(1)}, bf16[64,7168]{1,0:T(8,128)(2,1)S(1)}, u32[]{:S(2)}, u32[]{:S(2)}) %collective-permute-start.41) | collective-permute-done | bytes 917536 | tf_op jit(solution)/shard_map/ppermute | solution.py:54
  198.2 6.8 %collective-permute-done.52 = bf16[64,7168]{1,0:T(8,128)(2,1)S(1)} collective-permute-done((bf16[64,7168]{1,0:T(8,128)(2,1)S(1)}, bf16[64,7168]{1,0:T(8,128)(2,1)S(1)}, u32[]{:S(2)}, u32[]{:S(2)}) %collective-permute-start.52) | collective-permute-done | bytes 917536 | tf_op jit(solution)/shard_map/ppermute | solution.py:54
  208.1 6.7 %collective-permute-done.45 = bf16[16,7168]{1,0:T(8,128)(2,1)S(1)} collective-permute-done((bf16[16,7168]{1,0:T(8,128)(2,1)S(1)}, bf16[16,7168]{1,0:T(8,128)(2,1)S(1)}, u32[]{:S(2)}, u32[]{:S(2)}) %collective-permute-start.45) | collective-permute-done | bytes 229408 | tf_op jit(solution)/shard_map/ppermute | solution.py:54
  236.7 6.7 %collective-permute-done.54 = bf16[4,7168]{1,0:T(4,128)(2,1)S(1)} collective-permute-done((bf16[4,7168]{1,0:T(4,128)(2,1)S(1)}, bf16[4,7168]{1,0:T(4,128)(2,1)S(1)}, u32[]{:S(2)}, u32[]{:S(2)}) %collective-permute-start.54) | collective-permute-done | bytes 57376 | tf_op jit(solution)/shard_map/ppermute | solution.py:54
  283.8 8.6 %collective-permute-done.77 = bf16[4,7296]{1,0:T(4,128)(2,1)S(1)} collective-permute-done((bf16[4,7296]{1,0:T(4,128)(2,1)S(1)}, bf16[4,7296]{1,0:T(4,128)(2,1)S(1)}, u32[]{:S(2)}, u32[]{:S(2)}) %collective-permute-start.77) | collective-permute-done | bytes 58400 | tf_op jit(solution)/shard_map/ppermute | solution.py:54
  321.3 13.4 %shard_map.135 = (bf16[64,7168]{1,0:T(8,128)(2,1)S(1)}, bf16[64,7168]{1,0:T(8,128)(2,1)S(1)}, bf16[32,7168]{1,0:T(8,128)(2,1)S(1)}, bf16[64,7168]{1,0:T(8,128)(2,1)S(1)}) custom-call(s32[2]{0:T(128)S(1)} %pad_add_fusion.expert_ref, bf16[64,7296]{1,0:T(8,128)(2,1)S(1)} %pad_maximum_fusion.2.refs_0_.refs_4_, ...), custom_call_target="tpu_custom_call" | custom-call | flops 4932501504 | bytes 28442624 | tf_op jit(solution)/shard_map/pallas_call | solution.py:162
  338.3 12.7 %shard_map.136 = (bf16[64,7168]{1,0:T(8,128)(2,1)S(1)}, bf16[64,7168]{1,0:T(8,128)(2,1)S(1)}, bf16[64,7168]{1,0:T(8,128)(2,1)S(1)}) custom-call(s32[2]{0:T(128)S(1)} %pad_add_fusion.expert_ref, bf16[64,7296]{1,0:T(8,128)(2,1)S(1)} %collective-permute-done.88.refs_0_.refs_3_, bf16[64,7296]{1,0:T(8,128)(2,1)S(1)} %collective-permute-done.89.refs_1_.refs_4_, ...), custom_call_target="tpu_custom_call" | custom-call | flops 4227858432 | bytes 27525120 | tf_op jit(solution)/shard_map/pallas_call | solution.py:162
  354.4 12.7 %shard_map.137 = (bf16[64,7168]{1,0:T(8,128)(2,1)S(1)}, bf16[64,7168]{1,0:T(8,128)(2,1)S(1)}, bf16[64,7168]{1,0:T(8,128)(2,1)S(1)}) custom-call(s32[2]{0:T(128)S(1)} %pad_add_fusion.expert_ref, bf16[64,7296]{1,0:T(8,128)(2,1)S(1)} %collective-permute-done.91.refs_0_.refs_3_, bf16[64,7296]{1,0:T(8,128)(2,1)S(1)} %collective-permute-done.92.refs_1_.refs_4_, ...), custom_call_target="tpu_custom_call" | custom-call | flops 4227858432 | bytes 27525120 | tf_op jit(solution)/shard_map/pallas_call | solution.py:162
  369.1 12.2 %shard_map.138 = (bf16[64,7168]{1,0:T(8,128)(2,1)S(1)}, bf16[64,7168]{1,0:T(8,128)(2,1)S(1)}, bf16[32,7168]{1,0:T(8,128)(2,1)S(1)}) custom-call(s32[2]{0:T(128)S(1)} %pad_add_fusion.expert_ref, bf16[64,7296]{1,0:T(8,128)(2,1)S(1)} %collective-permute-done.93.refs_0_.refs_3_, bf16[64,7296]{1,0:T(8,128)(2,1)S(1)} %collective-permute-done.94.refs_1_.refs_4_, ...), custom_call_target="tpu_custom_call" | custom-call | flops 3523215360 | bytes 26607616 | tf_op jit(solution)/shard_map/pallas_call | solution.py:162
  390.1 5.7 %collective-permute-done.97 = bf16[64,7168]{1,0:T(8,128)(2,1)S(1)} collective-permute-done((bf16[64,7168]{1,0:T(8,128)(2,1)S(1)}, bf16[64,7168]{1,0:T(8,128)(2,1)S(1)}, u32[]{:S(2)}, u32[]{:S(2)}) %collective-permute-start.97) | collective-permute-done | bytes 917536 | tf_op jit(solution)/shard_map/ppermute | solution.py:54
  406.2 6.2 %collective-permute-done.99 = bf16[64,7168]{1,0:T(8,128)(2,1)S(1)} collective-permute-done((bf16[64,7168]{1,0:T(8,128)(2,1)S(1)}, bf16[64,7168]{1,0:T(8,128)(2,1)S(1)}, u32[]{:S(2)}, u32[]{:S(2)}) %collective-permute-start.99) | collective-permute-done | bytes 917536 | tf_op jit(solution)/shard_map/ppermute | solution.py:54
  425.7 7.1 %collective-permute-done.102 = bf16[64,7168]{1,0:T(8,128)(2,1)S(1)} collective-permute-done((bf16[64,7168]{1,0:T(8,128)(2,1)S(1)}, bf16[64,7168]{1,0:T(8,128)(2,1)S(1)}, u32[]{:S(2)}, u32[]{:S(2)}) %collective-permute-start.102) | collective-permute-done | bytes 917536 | tf_op jit(solution)/shard_map/ppermute | solution.py:54
  437.9 8.3 %collective-permute-done.104 = bf16[64,7168]{1,0:T(8,128)(2,1)S(1)} collective-permute-done((bf16[64,7168]{1,0:T(8,128)(2,1)S(1)}, bf16[64,7168]{1,0:T(8,128)(2,1)S(1)}, u32[]{:S(2)}, u32[]{:S(2)}) %collective-permute-start.104) | collective-permute-done | bytes 917536 | tf_op jit(solution)/shard_map/ppermute | solution.py:54
  471.2 7.0 %collective-permute-done.107 = bf16[32,7168]{1,0:T(8,128)(2,1)S(1)} collective-permute-done((bf16[32,7168]{1,0:T(8,128)(2,1)S(1)}, bf16[32,7168]{1,0:T(8,128)(2,1)S(1)}, u32[]{:S(2)}, u32[]{:S(2)}) %collective-permute-start.107) | collective-permute-done | bytes 458784 | tf_op jit(solution)/shard_map/ppermute | solution.py:54
  503.7 5.4 %collective-permute-done.115 = bf16[4,7168]{1,0:T(4,128)(2,1)S(1)} collective-permute-done((bf16[4,7168]{1,0:T(4,128)(2,1)S(1)}, bf16[4,7168]{1,0:T(4,128)(2,1)S(1)}, u32[]{:S(2)}, u32[]{:S(2)}) %collective-permute-start.115) | collective-permute-done | bytes 57376 | tf_op jit(solution)/shard_map/ppermute | solution.py:54
  (465 shorter events, 295.4 us)
Async XLA Ops:
  11.7 41.8 %collective-permute-start.27 = (bf16[1,7168,256]{2,1,0:T(8,128)(2,1)}, bf16[1,7168,256]{2,1,0:T(8,128)(2,1)}, u32[]{:S(2)}, u32[]{:S(2)}) collective-permute-start(bf16[1,7168,256]{2,1,0:T(8,128)(2,1)} %refs_8_.15), channel_id=1, source_target_pairs={{0,1},{1,0},{64,65},{65,64},{128,129},{129,128},{192,193},{193,192... | collective-permute-start | bytes 11010056 | tf_op jit(solution)/shard_map/ppermute | solution.py:42
  26.8 20.7 %collective-permute-start.9 = (bf16[32,7296]{1,0:T(8,128)(2,1)S(1)}, bf16[32,7296]{1,0:T(8,128)(2,1)S(1)}, u32[]{:S(2)}, u32[]{:S(2)}) collective-permute-start(bf16[32,7296]{1,0:T(8,128)(2,1)S(1)} %concatenate.110.refs_2_.refs_6_), channel_id=1, source_target_pairs={{0,1},{1,0},{64,65},{65,64},{128,129},{129,128},{192,193},{193,192... | collective-permute-start | bytes 1400840 | tf_op jit(solution)/shard_map/ppermute | solution.py:42
  53.6 22.4 %collective-permute-start.28 = (bf16[1,256,7168]{2,1,0:T(8,128)(2,1)}, bf16[1,256,7168]{2,1,0:T(8,128)(2,1)}, u32[]{:S(2)}, u32[]{:S(2)}) collective-permute-start(bf16[1,256,7168]{2,1,0:T(8,128)(2,1)} %refs_10_.15), channel_id=1, source_target_pairs={{0,1},{1,0},{64,65},{65,64},{128,129},{129,128},{192,193},{193,192... | collective-permute-start | bytes 11010056 | tf_op jit(solution)/shard_map/ppermute | solution.py:42
  73.1 21.8 %collective-permute-start.21 = (bf16[64,7296]{1,0:T(8,128)(2,1)S(1)}, bf16[64,7296]{1,0:T(8,128)(2,1)}, u32[]{:S(2)}, u32[]{:S(2)}) collective-permute-start(bf16[64,7296]{1,0:T(8,128)(2,1)S(1)} %pad_maximum_fusion.refs_0_.refs_4_), channel_id=1, source_target_pairs={{0,1},{1,0},{64,65},{65,64},{128,129},{129,128},{192,193},{193,192... | collective-permute-start | bytes 2801672 | tf_op jit(solution)/shard_map/ppermute | solution.py:42
  73.2 21.7 %collective-permute-start.24 = (bf16[64,7296]{1,0:T(8,128)(2,1)S(1)}, bf16[64,7296]{1,0:T(8,128)(2,1)S(1)}, u32[]{:S(2)}, u32[]{:S(2)}) collective-permute-start(bf16[64,7296]{1,0:T(8,128)(2,1)S(1)} %pad_maximum_fusion.refs_0_.refs_4_), channel_id=1, source_target_pairs={{0,16},{1,49},{64,80},{65,113},{128,144},{129,177},{192,208},{193,... | collective-permute-start | bytes 2801672 | tf_op jit(solution)/shard_map/ppermute | solution.py:54
  74.4 20.5 %collective-permute-start.22 = (bf16[64,7296]{1,0:T(8,128)(2,1)S(1)}, bf16[64,7296]{1,0:T(8,128)(2,1)}, u32[]{:S(2)}, u32[]{:S(2)}) collective-permute-start(bf16[64,7296]{1,0:T(8,128)(2,1)S(1)} %pad_maximum_fusion.1.refs_1_.refs_5_), channel_id=1, source_target_pairs={{0,1},{1,0},{64,65},{65,64},{128,129},{129,128},{192,193},{193,192... | collective-permute-start | bytes 2801672 | tf_op jit(solution)/shard_map/ppermute | solution.py:42
  74.9 20.0 %collective-permute-start.23 = (bf16[64,7296]{1,0:T(8,128)(2,1)}, bf16[64,7296]{1,0:T(8,128)(2,1)}, u32[]{:S(2)}, u32[]{:S(2)}) collective-permute-start(bf16[64,7296]{1,0:T(8,128)(2,1)} %collective-permute-done.20.refs_3_.refs_7_), channel_id=1, source_target_pairs={{0,64},{1,195},{64,128},{65,1},{128,192},{129,65},{192,2},{193,129... | collective-permute-start | bytes 2801672 | tf_op jit(solution)/shard_map/ppermute | solution.py:54
  76.0 18.9 %collective-permute-start.25 = (bf16[64,7296]{1,0:T(8,128)(2,1)S(1)}, bf16[64,7296]{1,0:T(8,128)(2,1)}, u32[]{:S(2)}, u32[]{:S(2)}) collective-permute-start(bf16[64,7296]{1,0:T(8,128)(2,1)S(1)} %pad_maximum_fusion.1.refs_1_.refs_5_), channel_id=1, source_target_pairs={{0,4},{1,13},{64,68},{65,77},{128,132},{129,141},{192,196},{193,20... | collective-permute-start | bytes 2801672 | tf_op jit(solution)/shard_map/ppermute | solution.py:54
  227.4 16.0 %collective-permute-start.55 = (bf16[8,7168]{1,0:T(8,128)(2,1)S(1)}, bf16[8,7168]{1,0:T(8,128)(2,1)S(1)}, u32[]{:S(2)}, u32[]{:S(2)}) collective-permute-start(bf16[8,7168]{1,0:T(8,128)(2,1)S(1)} %get-tuple-element.241), channel_id=1, source_target_pairs={{0,194},{1,65},{64,0},{65,129},{128,64},{129,193},{192,128},{193,3... | collective-permute-start | bytes 344072 | tf_op jit(solution)/shard_map/ppermute | solution.py:54
  274.9 22.5 %collective-permute-start.73 = (bf16[32,7296]{1,0:T(8,128)(2,1)S(1)}, bf16[32,7296]{1,0:T(8,128)(2,1)S(1)}, u32[]{:S(2)}, u32[]{:S(2)}) collective-permute-start(bf16[32,7296]{1,0:T(8,128)(2,1)S(1)} %concatenate.126.refs_2_.refs_6_), channel_id=1, source_target_pairs={{0,1},{1,0},{64,65},{65,64},{128,129},{129,128},{192,193},{193,192... | collective-permute-start | bytes 1400840 | tf_op jit(solution)/shard_map/ppermute | solution.py:42
  275.1 17.4 %collective-permute-start.74 = (bf16[8,7296]{1,0:T(8,128)(2,1)S(1)}, bf16[8,7296]{1,0:T(8,128)(2,1)S(1)}, u32[]{:S(2)}, u32[]{:S(2)}) collective-permute-start(bf16[8,7296]{1,0:T(8,128)(2,1)S(1)} %pad_maximum_fusion.20), channel_id=1, source_target_pairs={{0,64},{1,195},{64,128},{65,1},{128,192},{129,65},{192,2},{193,129... | collective-permute-start | bytes 350216 | tf_op jit(solution)/shard_map/ppermute | solution.py:54
  316.8 18.7 %collective-permute-start.85 = (bf16[64,7296]{1,0:T(8,128)(2,1)S(1)}, bf16[64,7296]{1,0:T(8,128)(2,1)S(1)}, u32[]{:S(2)}, u32[]{:S(2)}) collective-permute-start(bf16[64,7296]{1,0:T(8,128)(2,1)S(1)} %pad_maximum_fusion.2.refs_0_.refs_4_), channel_id=1, source_target_pairs={{0,1},{1,0},{64,65},{65,64},{128,129},{129,128},{192,193},{193,192... | collective-permute-start | bytes 2801672 | tf_op jit(solution)/shard_map/ppermute | solution.py:42
  316.8 18.7 %collective-permute-start.86 = (bf16[64,7296]{1,0:T(8,128)(2,1)S(1)}, bf16[64,7296]{1,0:T(8,128)(2,1)S(1)}, u32[]{:S(2)}, u32[]{:S(2)}) collective-permute-start(bf16[64,7296]{1,0:T(8,128)(2,1)S(1)} %pad_maximum_fusion.3.refs_1_.refs_5_), channel_id=1, source_target_pairs={{0,1},{1,0},{64,65},{65,64},{128,129},{129,128},{192,193},{193,192... | collective-permute-start | bytes 2801672 | tf_op jit(solution)/shard_map/ppermute | solution.py:42
  317.3 18.2 %collective-permute-start.87 = (bf16[64,7296]{1,0:T(8,128)(2,1)S(1)}, bf16[64,7296]{1,0:T(8,128)(2,1)S(1)}, u32[]{:S(2)}, u32[]{:S(2)}) collective-permute-start(bf16[64,7296]{1,0:T(8,128)(2,1)S(1)} %collective-permute-done.84.refs_3_.refs_7_), channel_id=1, source_target_pairs={{0,64},{1,195},{64,128},{65,1},{128,192},{129,65},{192,2},{193,129... | collective-permute-start | bytes 2801672 | tf_op jit(solution)/shard_map/ppermute | solution.py:54
  318.9 16.6 %collective-permute-start.88 = (bf16[64,7296]{1,0:T(8,128)(2,1)S(1)}, bf16[64,7296]{1,0:T(8,128)(2,1)S(1)}, u32[]{:S(2)}, u32[]{:S(2)}) collective-permute-start(bf16[64,7296]{1,0:T(8,128)(2,1)S(1)} %pad_maximum_fusion.2.refs_0_.refs_4_), channel_id=1, source_target_pairs={{0,16},{1,49},{64,80},{65,113},{128,144},{129,177},{192,208},{193,... | collective-permute-start | bytes 2801672 | tf_op jit(solution)/shard_map/ppermute | solution.py:54
  351.1 18.0 %collective-permute-start.93 = (bf16[64,7296]{1,0:T(8,128)(2,1)S(1)}, bf16[64,7296]{1,0:T(8,128)(2,1)S(1)}, u32[]{:S(2)}, u32[]{:S(2)}) collective-permute-start(bf16[64,7296]{1,0:T(8,128)(2,1)S(1)} %collective-permute-done.88.refs_0_.refs_3_), channel_id=1, source_target_pairs={{0,16},{1,49},{64,80},{65,113},{128,144},{129,177},{192,208},{193,... | collective-permute-start | bytes 2801672 | tf_op jit(solution)/shard_map/ppermute | solution.py:54
  351.9 17.2 %collective-permute-start.94 = (bf16[64,7296]{1,0:T(8,128)(2,1)S(1)}, bf16[64,7296]{1,0:T(8,128)(2,1)S(1)}, u32[]{:S(2)}, u32[]{:S(2)}) collective-permute-start(bf16[64,7296]{1,0:T(8,128)(2,1)S(1)} %collective-permute-done.89.refs_1_.refs_4_), channel_id=1, source_target_pairs={{0,4},{1,13},{64,68},{65,77},{128,132},{129,141},{192,196},{193,20... | collective-permute-start | bytes 2801672 | tf_op jit(solution)/shard_map/ppermute | solution.py:54
  352.7 16.4 %collective-permute-start.95 = (bf16[32,7296]{1,0:T(8,128)(2,1)S(1)}, bf16[32,7296]{1,0:T(8,128)(2,1)S(1)}, u32[]{:S(2)}, u32[]{:S(2)}) collective-permute-start(bf16[32,7296]{1,0:T(8,128)(2,1)S(1)} %slice.368), channel_id=1, source_target_pairs={{0,64},{1,195},{64,128},{65,1},{128,192},{129,65},{192,2},{193,129... | collective-permute-start | bytes 1400840 | tf_op jit(solution)/shard_map/ppermute | solution.py:54
  421.0 29.8 %collective-permute-start = (bf16[72,576]{1,0:T(8,128)(2,1)}, bf16[72,576]{1,0:T(8,128)(2,1)S(1)}, u32[]{:S(2)}, u32[]{:S(2)}) collective-permute-start(bf16[72,576]{1,0:T(8,128)(2,1)} %concatenate.105), channel_id=1, source_target_pairs={{0,192},{64,0},{128,64},{192,128},{1,193},{65,1},{129,65},{193,129... | collective-permute-start | bytes 248840 | tf_op jit(solution)/shard_map/ppermute | solution.py:329
  422.3 29.8 %collective-permute-start.1 = (bf16[72,576]{1,0:T(8,128)(2,1)}, bf16[72,576]{1,0:T(8,128)(2,1)}, u32[]{:S(2)}, u32[]{:S(2)}) collective-permute-start(bf16[72,576]{1,0:T(8,128)(2,1)} %concatenate.105), channel_id=1, source_target_pairs={{0,128},{64,192},{128,0},{192,64},{1,129},{65,193},{129,1},{193,65... | collective-permute-start | bytes 248840 | tf_op jit(solution)/shard_map/ppermute | solution.py:329
  424.3 29.6 %collective-permute-start.2 = (bf16[72,576]{1,0:T(8,128)(2,1)}, bf16[72,576]{1,0:T(8,128)(2,1)}, u32[]{:S(2)}, u32[]{:S(2)}) collective-permute-start(bf16[72,576]{1,0:T(8,128)(2,1)} %concatenate.105), channel_id=1, source_target_pairs={{0,64},{64,128},{128,192},{192,0},{1,65},{65,129},{129,193},{193,1... | collective-permute-start | bytes 248840 | tf_op jit(solution)/shard_map/ppermute | solution.py:329
  461.9 17.6 %collective-permute-start.114 = (bf16[32,7168]{1,0:T(8,128)(2,1)S(1)}, bf16[32,7168]{1,0:T(8,128)(2,1)S(1)}, u32[]{:S(2)}, u32[]{:S(2)}) collective-permute-start(bf16[32,7168]{1,0:T(8,128)(2,1)S(1)} %slice.464), channel_id=1, source_target_pairs={{0,1},{1,0},{64,65},{65,64},{128,129},{129,128},{192,193},{193,192... | collective-permute-start | bytes 1376264 | tf_op jit(solution)/shard_map/ppermute | solution.py:42
  492.6 16.5 %collective-permute-start.116 = (bf16[8,7168]{1,0:T(8,128)(2,1)S(1)}, bf16[8,7168]{1,0:T(8,128)(2,1)S(1)}, u32[]{:S(2)}, u32[]{:S(2)}) collective-permute-start(bf16[8,7168]{1,0:T(8,128)(2,1)S(1)} %get-tuple-element.238), channel_id=1, source_target_pairs={{0,194},{1,65},{64,0},{65,129},{128,64},{129,193},{192,128},{193,3... | collective-permute-start | bytes 344072 | tf_op jit(solution)/shard_map/ppermute | solution.py:54
  493.3 15.9 %collective-permute-start.117 = (bf16[8,7168]{1,0:T(8,128)(2,1)S(1)}, bf16[8,7168]{1,0:T(8,128)(2,1)S(1)}, u32[]{:S(2)}, u32[]{:S(2)}) collective-permute-start(bf16[8,7168]{1,0:T(8,128)(2,1)S(1)} %get-tuple-element.240), channel_id=1, source_target_pairs={{0,130},{1,129},{64,194},{65,193},{128,0},{129,3},{192,64},{193,67... | collective-permute-start | bytes 344072 | tf_op jit(solution)/shard_map/ppermute | solution.py:54
  (133 other events, 1376.0 us)
